TPU v7x, 32 devices: a whole 2x2x4 slice. The times are simulated.
32 devices in a mesh: panel: 8 (over y, x, core), col: 4 (over z).
Axes of the slice: x: 2, y: 2, z: 4, core: 2. Of those that a mesh axis runs over, the one named last changes fastest.
Arguments:
- panel_rows: bfloat16 [16384, 512], P(('panel', 'col')), may hold values from -6 to 6
- diag_blocks: float32 [512, 512], replicated
- adjoint: bfloat16 [16384, 16384], P('panel', 'col')
- fill: int32 [64, 64], P('panel', 'col'), may hold values from 0 to 1, as said below
Outputs:
- grad_panel: float32 [16384, 512], P(('panel', 'col'))
- grad_diag: float32 [512, 512], replicated
Inputs may be any that keep to these rules, and one draw needn't show every extreme that they name: fill is 1 on every diagonal block, fill equals its transpose, and adjoint equals its transpose.
All inputs are finite; a program needn't handle non-finite values.
Results may differ from a plain program's by a relative error of at most 0.004.
Values may be sent and summed in bfloat16 or wider, within the bound.
A program may use at most 128 MiB of HBM per device.

v0:
```python
import jax
import jax.numpy as jnp
from jax import lax
from jax.sharding import PartitionSpec as P

B = 256


def broadcast(shard, axis, root):
    mine = lax.axis_index(axis) == root
    return lax.psum(jnp.where(mine, shard, jnp.zeros_like(shard)), axis)


def factor_with_logdet(matrix):
    lower = jnp.linalg.cholesky(matrix)
    return (lower, 2.0 * jnp.sum(jnp.log(jnp.diagonal(lower))))


def shards(panel_rows, diag_blocks, adjoint, fill):
    lower = jnp.linalg.cholesky(diag_blocks)
    scaled = jax.scipy.linalg.solve_triangular(
        lower, panel_rows.astype(jnp.float32).T, lower=True
    ).T.astype(jnp.bfloat16)
    piece = scaled.shape[0]
    n_col = lax.axis_size("col")
    n_pan = lax.axis_size("panel")
    groups = n_pan // n_col
    panel_block = lax.all_gather(scaled, "col", axis=0, tiled=True)
    parts = []
    for offset in range(groups):
        root = lax.axis_index("col") * groups + offset
        parts.append(broadcast(panel_block, "panel", root))
    columns = jnp.concatenate(parts, 0)
    row_fill = jnp.repeat(fill, B, axis=0)
    col_blocks = fill.shape[1]
    marks = row_fill.astype(jnp.bfloat16)
    masked = (
        adjoint.reshape(lax.axis_size("col") * piece, col_blocks, B) * marks[:, :, None]
    ).reshape(lax.axis_size("col") * piece, col_blocks * B)
    summed = lax.psum_scatter(
        jnp.dot(masked, columns, preferred_element_type=jnp.float32),
        "col",
        scatter_dimension=0,
        tiled=True,
    )
    grad_scaled = -summed
    grad_panel = jax.scipy.linalg.solve_triangular(lower, grad_scaled.T, lower=True, trans=1).T
    partial_lower = -jnp.dot(
        grad_panel.T, scaled.astype(jnp.float32), precision=lax.Precision.HIGHEST
    )
    grad_lower = jnp.tril(lax.psum(partial_lower, ("panel", "col")))
    outputs, pullback = jax.vjp(factor_with_logdet, diag_blocks)
    grad_diag = pullback((grad_lower, jnp.ones((), jnp.float32)))[0]
    return (grad_panel, grad_diag)


def solution(mesh):
    in_specs = (P(("panel", "col"), None), P(), P("panel", "col"), P("panel", "col"))
    out_specs = (P(("panel", "col"), None), P())
    return jax.shard_map(shards, mesh=mesh, in_specs=in_specs, out_specs=out_specs, check_vma=False)
```

profile of v0, /device:TPU:0, one launch (start us, length us, event | category | flops | bytes accessed | tf_op | source)
XLA Modules:
  0.0 562.0 jit_solution(4063525348366002639)
XLA Ops:
  7.2 1.6 copy.11
  8.8 1.4 fusion.8
  10.3 11.7 %custom-call.40 = f32[128,128]{1,0:T(8,128)S(1)} custom-call(f32[128,128]{1,0:T(8,128)S(1)} %slice.234), custom_call_target="Cholesky" | custom-call | tf_op jit(solution)/shard_map/jit(cholesky)/cholesky/custom-call.4 | solution.py:20
  22.0 9.8 %custom-call.41 = f32[1,128,128]{1,2,0:T(8,128)S(1)} custom-call(f32[1,128,128]{2,1,0:T(8,128)S(1)} %get-tuple-element.61), custom_call_target="InvertDiagBlocksLowerTriangular" | custom-call | tf_op jit(solution)/shard_map/jit(cholesky)/cholesky/custom-call.10 | solution.py:20
  32.9 11.7 %custom-call.42 = f32[128,128]{1,0:T(8,128)S(1)} custom-call(f32[128,128]{1,0:T(8,128)S(1)} %slice.238), custom_call_target="Cholesky" | custom-call | tf_op jit(solution)/shard_map/jit(cholesky)/cholesky/custom-call.5 | solution.py:20
  44.8 10.3 %custom-call.43 = f32[1,128,128]{1,2,0:T(8,128)S(1)} custom-call(f32[1,128,128]{2,1,0:T(8,128)S(1)} %get-tuple-element.58), custom_call_target="InvertDiagBlocksLowerTriangular" | custom-call | tf_op jit(solution)/shard_map/jit(cholesky)/cholesky/custom-call.11 | solution.py:20
  55.7 11.7 %custom-call.44 = f32[128,128]{1,0:T(8,128)S(1)} custom-call(f32[128,128]{1,0:T(8,128)S(1)} %slice.243), custom_call_target="Cholesky" | custom-call | tf_op jit(solution)/shard_map/jit(cholesky)/cholesky/custom-call.6 | solution.py:20
  67.5 9.8 %custom-call.45 = f32[1,128,128]{1,2,0:T(8,128)S(1)} custom-call(f32[1,128,128]{2,1,0:T(8,128)S(1)} %get-tuple-element.55), custom_call_target="InvertDiagBlocksLowerTriangular" | custom-call | tf_op jit(solution)/shard_map/jit(cholesky)/cholesky/custom-call.12 | solution.py:20
  77.9 11.9 %custom-call.46 = f32[128,128]{1,0:T(8,128)S(1)} custom-call(f32[128,128]{1,0:T(8,128)S(1)} %convolution_subtract_fusion.14), custom_call_target="Cholesky" | custom-call | tf_op jit(solution)/shard_map/jit(cholesky)/cholesky/custom-call.7 | solution.py:20
  94.5 8.5 %while.5 = (s32[]{:T(128)}, f32[512,512]{1,0:T(8,128)S(1)}, s32[4,2]{0,1:T(2,128)S(1)}, f32[4,128,128]{2,1,0:T(8,128)S(1)}, s32[]{:T(128)}) while((s32[]{:T(128)}, f32[512,512]{1,0:T(8,128)S(1)}, s32[4,2]{0,1:T(2,128)S(1)}, f32[4,128,128]{2,1,0:T(8,128)S(1)}, s32[]{:T(128)}) %tuple.53), condition=%wide.while_cond, body=%wide.while_body.sunk | while | flops 2 | bytes 131189 | solution.py:47
  95.2 1.4 bitcast_dynamic-update-slice_fusion.2
  97.3 1.4 bitcast_dynamic-update-slice_fusion.2
  99.4 1.4 bitcast_dynamic-update-slice_fusion.2
  101.5 1.4 bitcast_dynamic-update-slice_fusion.2
  103.0 39.3 %custom-call.47 = f32[4,128,128]{1,2,0:T(8,128)S(1)} custom-call(f32[4,128,128]{2,1,0:T(8,128)S(1)} %get-tuple-element.32), custom_call_target="InvertDiagBlocksLowerTriangular" | custom-call | tf_op jit(solution)/shard_map/jit(_solve_triangular)/triangular_solve/custom-call.0 | solution.py:47
  145.2 1.5 convolution_subtract_fusion.11
  148.1 48.7 %all-gather.2.cloned.1.call-done = bf16[2048,512]{0,1:T(8,128)(2,1)} async-done(((bf16[512,512]{0,1:T(8,128)(2,1)}), bf16[2048,512]{0,1:T(8,128)(2,1)}) %all-gather.2.cloned.1.call-update) | async-done | bytes 2097168 | tf_op jit(solution)/shard_map/all_gather | solution.py:28
  196.8 3.8 broadcast_select_fusion.1
  201.0 4.9 mul.15
  205.9 10.7 %copy.16 = bf16[256,8,16,256]{3,1,2,0:T(8,128)(2,1)} copy(bf16[256,8,16,256]{3,2,1,0:T(8,128)(2,1)S(1)} %bitcast.113) | data formatting | bytes 33554432
  216.6 64.1 %all-reduce.7.cloned.1.call-done = (bf16[2048,512]{0,1:T(8,128)(2,1)}, bf16[2048,512]{0,1:T(8,128)(2,1)}) async-done(((bf16[2048,512]{0,1:T(8,128)(2,1)}, bf16[2048,512]{0,1:T(8,128)(2,1)}), (bf16[2048,512]{0,1:T(8,128)(2,1)}, bf16[2048,512]{0,1:T(8,128)(2,1)})) %all-reduce.7.cloned.1.call-update) | async-done | bytes 4194320 | tf_op jit(solution)/shard_map/psum | solution.py:11
  280.7 17.6 %fusion = f32[2048,512]{1,0:T(8,128)} fusion(bf16[2048,4096]{1,0:T(8,128)(2,1)} %param.9, bf16[2048,4096]{1,0:T(8,128)(2,1)} %bitcast.116, bf16[2048,512]{0,1:T(8,128)(2,1)} %get-tuple-element.46, bf16[2048,512]{0,1:T(8,128)(2,1)} %get-tuple-element.47), kind=kOutput, calls=%fused_computation.4 | convolution fusion | flops 8606711808 | bytes 41943040 | tf_op jit(solution)/shard_map/dot_general | solution.py:41
  298.3 76.9 %reduce-scatter.2.cloned.1.call-done = f32[512,512]{1,0:T(8,128)} async-done(((f32[2048,512]{1,0:T(8,128)}), f32[512,512]{1,0:T(8,128)}) %reduce-scatter.2.cloned.1.call-update) | async-done | bytes 1048592 | tf_op jit(solution)/shard_map/reduce_scatter | solution.py:40
  379.3 1.5 convolution_subtract_fusion.10
  381.2 3.0 convolution_negate_fusion
  384.3 4.8 gather_fusion
  390.1 2.5 copy.15
  392.7 122.1 %all-reduce.5.cloned.1.call-done = f32[512,512]{1,0:T(8,128)} async-done(((f32[512,512]{1,0:T(8,128)}), f32[512,512]{1,0:T(8,128)}) %all-reduce.5.cloned.1.call-update) | async-done | bytes 1048592 | tf_op jit(solution)/shard_map/psum | solution.py:51
  514.8 1.4 fusion.10
  516.1 26.0 %scatter_fusion = f32[512,512]{1,0:T(8,128)S(1)} fusion(f32[512,512]{1,0:T(8,128)S(1)} %fusion.10, s32[512]{0:T(512)S(1)} %bitcast.114, f32[512]{0:T(512)S(1)} %broadcast_divide_fusion), kind=kCustom, calls=%fused_computation.1 | custom fusion | flops 512 | bytes 10240 | tf_op jit(solution)/shard_map/transpose(jvp(jit(diagonal)))/cond/branch_0_fun/scatter-add | solution.py:16
  542.2 1.9 fusion.5
  550.0 1.5 convolution_subtract_fusion.8
  (92 shorter events, 26.8 us)
Async XLA Ops:
  7.2 189.6 %all-gather.2.cloned.1.call-start = ((), (), s32[]{:S(2)}) async-start(), calls=%async_computation.1 | async-start | bytes 2621440 | tf_op jit(solution)/shard_map/all_gather | solution.py:28
  22.0 120.3 %copy-start.1 = (bf16[512,512]{1,0:T(8,128)(2,1)S(1)}, bf16[512,512]{1,0:T(8,128)(2,1)}, u32[]{:S(2)}) copy-start(bf16[512,512]{1,0:T(8,128)(2,1)} %param.7) | copy-start | bytes 1572868
  142.8 57.8 %copy-start.2 = (bf16[128,512]{1,0:T(8,128)(2,1)}, bf16[128,512]{1,0:T(8,128)(2,1)S(1)}, u32[]{:S(2)}) copy-start(bf16[128,512]{1,0:T(8,128)(2,1)S(1)} %get-tuple-element.66) | copy-start | bytes 393220
  143.8 56.8 %copy-start.3 = (bf16[128,512]{1,0:T(8,128)(2,1)}, bf16[128,512]{1,0:T(8,128)(2,1)S(1)}, u32[]{:S(2)}) copy-start(bf16[128,512]{1,0:T(8,128)(2,1)S(1)} %get-tuple-element.64) | copy-start | bytes 393220
  145.2 1.9 copy-start.4
  148.0 132.7 %all-reduce.7.cloned.1.call-start = ((), (), s32[]{:S(2)}) async-start(), calls=%async_computation.4 | async-start | bytes 8388608 | tf_op jit(solution)/shard_map/psum | solution.py:11
  148.0 52.8 %copy-start.5 = (s32[8,16]{1,0:T(8,128)S(1)}, s32[8,16]{1,0:T(8,128)}, u32[]{:S(2)}) copy-start(s32[8,16]{1,0:T(8,128)} %param.10) | copy-start | bytes 1540
  200.6 174.6 %reduce-scatter.2.cloned.1.call-start = ((), (), s32[]{:S(2)}) async-start(), calls=%async_computation.2 | async-start | bytes 5242880 | tf_op jit(solution)/shard_map/reduce_scatter | solution.py:40
  298.3 216.5 %all-reduce.5.cloned.1.call-start = ((), (), s32[]{:S(2)}) async-start(), calls=%async_computation.3 | async-start | bytes 2097152 | tf_op jit(solution)/shard_map/psum | solution.py:51
  550.0 1.9 copy-start
Sparse Core Ops, SparseCore 0:
  148.1 48.6 all-gather.1
  200.7 79.9 all-reduce.6
  298.4 76.8 reduce-scatter.1
  384.4 130.3 all-reduce.4
where the time goes:
time: 571 us; the launch traced here: 562 us
  waiting for transfers between devices  312 us (55%)
  other arithmetic  157 us (27%)
  matrix products  41.4 us (7%)
  local copies, waits for them, and re-layouts  33.9 us (6%)
  between operations  17.3 us (3%)
    psum x1, waiting for transfers between devices, shards(): grad_lower = jnp.tril(lax.psum(partial_lower, ('panel', 'col')))  122 us
    another operation x14, other arithmetic, shards(): lower = jnp.linalg.cholesky(diag_blocks)  79 us
    reduce_scatter x1, waiting for transfers between devices, shards(): lax.psum_scatter(jnp.dot(masked, columns, preferred_element_type=jnp.floa...  76.9 us
    psum x1, waiting for transfers between devices, broadcast(): return lax.psum(jnp.where(mine, shard, jnp.zeros_like(shard)), axis)  64.1 us
    all_gather x1, waiting for transfers between devices, shards(): panel_block = lax.all_gather(scaled, 'col', axis=0, tiled=True)  48.7 us
    another operation x4, other arithmetic, shards(): jax.scipy.linalg.solve_triangular(lower, grad_scaled.T, lower=True, trans=1)  39.4 us
    scatter-add x1, other arithmetic, factor_with_logdet(): return (lower, 2.0 * jnp.sum(jnp.log(jnp.diagonal(lower))))  26 us
    dot_general x1, matrix products, shards(): jnp.dot(masked, columns, preferred_element_type=jnp.float32)  17.6 us
  transfers between devices with their start and end apart: 4, of which 4 were waited for; matrix products, arithmetic and copies ran while one was open for 4% of the time, Pallas kernels for 0%

commit v1 on v0

v1 whole, which is shorter than its diff:
```python
import functools

import jax
import jax.numpy as jnp
from jax import lax
from jax.experimental import pallas as pl
from jax.experimental.pallas import tpu as pltpu
from jax.sharding import PartitionSpec as P

B = 256
HIGHEST = lax.Precision.HIGHEST


def inverse_kernel(matrix_ref, out_ref, scaled_ref, x_ref, res_ref):
    n = matrix_ref.shape[0]
    rows = lax.broadcasted_iota(jnp.int32, (n, n), 0)
    cols = lax.broadcasted_iota(jnp.int32, (n, n), 1)
    eye = (rows == cols).astype(jnp.float32)
    matrix = matrix_ref[...]
    only = matrix * eye
    by_row = lax.rsqrt(jnp.sum(only, axis=1, keepdims=True))
    by_col = lax.rsqrt(jnp.sum(only, axis=0, keepdims=True))
    scaled = matrix * by_row * by_col
    scaled_ref[...] = scaled
    bound = jnp.max(jnp.sum(jnp.abs(scaled), axis=1, keepdims=True))
    alpha = jnp.where(bound < 1.9, 1.0, 2.0 / (1.0 + bound))
    x_ref[...] = alpha * (2.0 * eye - alpha * scaled)

    def unfinished(carry):
        step, before, last = carry
        stalled = (last < 0.25) & (last > 0.5 * before)
        return (step < 80) & (last > 1e-6) & jnp.logical_not(stalled)

    def improve(carry):
        step, _, last = carry
        x = x_ref[...]
        res_ref[...] = eye - jnp.dot(
            scaled_ref[...], x, precision=HIGHEST, preferred_element_type=jnp.float32
        )
        res = res_ref[...]
        x_ref[...] = x + jnp.dot(x, res, precision=HIGHEST, preferred_element_type=jnp.float32)
        return step + 1, last, jnp.sum(res * res)

    lax.while_loop(unfinished, improve, (0, jnp.float32(1e30), jnp.float32(1e29)))
    out_ref[...] = x_ref[...] * by_row * by_col


def inverse(matrix):
    n = matrix.shape[0]
    return pl.pallas_call(
        inverse_kernel,
        out_shape=jax.ShapeDtypeStruct((n, n), jnp.float32),
        in_specs=[pl.BlockSpec(memory_space=pltpu.VMEM)],
        out_specs=pl.BlockSpec(memory_space=pltpu.VMEM),
        scratch_shapes=[pltpu.VMEM((n, n), jnp.float32)] * 3,
        compiler_params=pltpu.CompilerParams(vmem_limit_bytes=24 * 1024 * 1024),
        cost_estimate=pl.CostEstimate(
            flops=24 * 2 * n**3, bytes_accessed=8 * n * n, transcendentals=0
        ),
    )(matrix)


def shards(panel_rows, diag_blocks, adjoint, fill):
    n_col = lax.axis_size("col")
    n_pan = lax.axis_size("panel")
    groups = n_pan // n_col
    pairs = []
    for c in range(n_col):
        for k in range(groups):
            for z in range(n_col):
                pairs.append(((groups * c + k) * n_col + z, (k * n_col + z) * n_col + c))
    moved = lax.ppermute(panel_rows, ("panel", "col"), pairs)
    columns = lax.all_gather(moved, "panel", axis=0, tiled=True)
    matrix = 0.5 * (diag_blocks + diag_blocks.T)
    inv = inverse(matrix)
    marks = jnp.repeat(fill, B, axis=0).astype(jnp.bfloat16)
    rows, wide = adjoint.shape
    masked = (adjoint.reshape(rows, wide // B, B) * marks[:, :, None]).reshape(rows, wide)
    partial = jnp.dot(masked, columns, preferred_element_type=jnp.float32)
    product = lax.psum_scatter(
        partial.astype(jnp.bfloat16), "col", scatter_dimension=0, tiled=True
    )
    quad = lax.psum(
        jnp.dot(panel_rows.T, product, preferred_element_type=jnp.float32), ("panel", "col")
    )
    grad_panel = -jnp.dot(product.astype(jnp.float32), inv, precision=lax.Precision.HIGH)
    quad = 0.5 * (quad + quad.T)
    half = jnp.dot(quad, inv, precision=lax.Precision.HIGH)
    grad_diag = inv + 0.5 * jnp.dot(inv, half, precision=lax.Precision.HIGH)
    return (grad_panel, 0.5 * (grad_diag + grad_diag.T))


def solution(mesh):
    in_specs = (P(("panel", "col"), None), P(), P("panel", "col"), P("panel", "col"))
    out_specs = (P(("panel", "col"), None), P())
    return jax.shard_map(shards, mesh=mesh, in_specs=in_specs, out_specs=out_specs, check_vma=False)
```

time: 571 us -> 297 us (0.52)
  the two profiles are of different devices: /device:TPU:0 before, /device:TPU:9 now
where the time goes in v1:
time: 297 us; the launch traced here: 293 us
  waiting for transfers between devices  222 us (75%)
  matrix products  25 us (8%)
  local copies, waits for them, and re-layouts  19 us (6%)
  between operations  13.8 us (5%)
  Pallas kernels  8.1 us (3%)
  starting transfers between devices  3.34 us (1%)
    psum x1, waiting for transfers between devices, shards(): lax.psum(jnp.dot(panel_rows.T, product, preferred_element_type=jnp.float3...  123 us
    reduce_scatter x1, waiting for transfers between devices, shards(): lax.psum_scatter(partial.astype(jnp.bfloat16), 'col', scatter_dimension=0...  40.4 us
    ppermute x1, waiting for transfers between devices, shards(): moved = lax.ppermute(panel_rows, ('panel', 'col'), pairs)  34.2 us
    all_gather x1, waiting for transfers between devices, shards(): columns = lax.all_gather(moved, 'panel', axis=0, tiled=True)  23.6 us
    dot_general x1, matrix products, shards(): partial = jnp.dot(masked, columns, preferred_element_type=jnp.float32)  17.3 us
    unnamed x8, local copies, waits for them, and re-layouts  11.8 us
    pallas_call x1, Pallas kernels, inverse(): pl.pallas_call(inverse_kernel, out_shape=jax.ShapeDtypeStruct((n, n), jnp...  8.1 us
  transfers between devices with their start and end apart: 4, of which 4 were waited for; matrix products, arithmetic and copies ran while one was open for 6% of the time, Pallas kernels for 3%

profile of v1, /device:TPU:9, one launch (start us, length us, event | category | flops | bytes accessed | tf_op | source)
XLA Modules:
  0.0 293.0 jit_solution(16472952521655626474)
XLA Ops:
  7.2 0.0 all-gather.2.cloned.1.call-start
  7.2 3.0 %collective-permute-start = (bf16[512,512]{1,0:T(8,128)(2,1)}, bf16[512,512]{1,0:T(8,128)(2,1)S(1)}, u32[]{:S(2)}, u32[]{:S(2)}) collective-permute-start(bf16[512,512]{1,0:T(8,128)(2,1)} %param.4), channel_id=1, source_target_pairs={{0,0},{1,4},{2,8},{3,12},{4,16},{5,20},{6,24},{7,28},{8,1},{9,5},{... | collective-permute-start | bytes 1572872 | tf_op jit(solution)/shard_map/ppermute | solution.py:72
  10.3 34.2 %collective-permute-done = bf16[512,512]{1,0:T(8,128)(2,1)S(1)} collective-permute-done((bf16[512,512]{1,0:T(8,128)(2,1)}, bf16[512,512]{1,0:T(8,128)(2,1)S(1)}, u32[]{:S(2)}, u32[]{:S(2)}) %collective-permute-start) | collective-permute-done | bytes 524320 | tf_op jit(solution)/shard_map/ppermute | solution.py:72
  44.5 0.0 copy-start.2
  44.5 0.8 copy-done.2
  45.3 0.0 all-gather.2.cloned.1.call-update
  45.3 0.0 reduce-scatter.2.cloned.1.call-start
  45.4 0.7 convert_element_type.15
  46.1 0.1 broadcast_in_dim.4
  46.1 4.9 %mul.23 = bf16[2048,16,256]{2,1,0:T(8,128)(2,1)S(1)} broadcast(bf16[2048,16]{1,0:T(8,128)(2,1)S(1)} %bitcast.28), dimensions={0,1} | broadcast | bytes 16842752 | tf_op jit(solution)/shard_map/mul | solution.py:78
  51.1 10.6 %copy.13 = bf16[256,8,16,256]{3,1,2,0:T(8,128)(2,1)} copy(bf16[256,8,16,256]{3,2,1,0:T(8,128)(2,1)S(1)} %bitcast.26) | data formatting | bytes 33554432
  61.7 23.6 %all-gather.2.cloned.1.call-done = bf16[4096,512]{1,0:T(8,128)(2,1)} async-done(((bf16[512,512]{1,0:T(8,128)(2,1)}), bf16[4096,512]{1,0:T(8,128)(2,1)}) %all-gather.2.cloned.1.call-update) | async-done | bytes 4194320 | tf_op jit(solution)/shard_map/all_gather | solution.py:73
  85.3 0.0 copy-start
  85.3 17.3 %fusion.2 = bf16[2048,512]{1,0:T(8,128)(2,1)} fusion(bf16[4096,512]{1,0:T(8,128)(2,1)} %all-gather.2.cloned.1.call-done, bf16[2048,4096]{1,0:T(8,128)(2,1)} %param.6, bf16[2048,4096]{1,0:T(8,128)(2,1)} %bitcast.27), kind=kOutput, calls=%fused_computation.2 | convolution fusion | flops 8599371776 | bytes 39845888 | tf_op jit(solution)/shard_map/dot_general | solution.py:79
  102.6 0.0 reduce-scatter.2.cloned.1.call-update
  102.6 0.2 all-reduce.2.cloned.1.call-start
  102.9 0.0 copy-done
  102.9 0.3 copy.6
  103.2 0.2 fusion.10.matrix_ref
  103.4 40.4 %reduce-scatter.2.cloned.1.call-done = bf16[512,512]{1,0:T(8,128)(2,1)} async-done(((bf16[2048,512]{1,0:T(8,128)(2,1)}), bf16[512,512]{1,0:T(8,128)(2,1)}) %reduce-scatter.2.cloned.1.call-update) | async-done | bytes 524304 | tf_op jit(solution)/shard_map/reduce_scatter | solution.py:80
  143.8 2.7 convolution_bitcast_fusion
  146.5 0.0 all-reduce.2.cloned.1.call-update
  146.6 8.1 %shard_map.59 = f32[512,512]{1,0:T(8,128)S(1)} custom-call(f32[512,512]{1,0:T(8,128)S(1)} %fusion.10.matrix_ref), custom_call_target="tpu_custom_call" | custom-call | flops 6442450944 | bytes 2097152 | tf_op jit(solution)/shard_map/pallas_call | solution.py:50
  154.7 0.3 copy.10
  155.0 0.0 copy-done.1
  155.0 1.7 convolution_negate_fusion
  156.7 123.4 %all-reduce.2.cloned.1.call-done = f32[512,512]{0,1:T(8,128)} async-done(((f32[512,512]{0,1:T(8,128)}), f32[512,512]{0,1:T(8,128)}) %all-reduce.2.cloned.1.call-update) | async-done | bytes 1048592 | tf_op jit(solution)/shard_map/psum | solution.py:83
  280.1 1.6 copy.7
  281.7 2.2 fusion.8
  283.9 1.0 fusion.5
  284.9 0.3 copy.11
  285.3 1.2 fusion.6
  (1 shorter events, 0.0 us)
Async XLA Ops:
  7.2 78.1 %all-gather.2.cloned.1.call-start = ((), (), s32[]{:S(2)}) async-start(), calls=%async_computation.1 | async-start | bytes 4718592 | tf_op jit(solution)/shard_map/all_gather | solution.py:73
  7.2 37.3 %collective-permute-start = (bf16[512,512]{1,0:T(8,128)(2,1)}, bf16[512,512]{1,0:T(8,128)(2,1)S(1)}, u32[]{:S(2)}, u32[]{:S(2)}) collective-permute-start(bf16[512,512]{1,0:T(8,128)(2,1)} %param.4), channel_id=1, source_target_pairs={{0,0},{1,4},{2,8},{3,12},{4,16},{5,20},{6,24},{7,28},{8,1},{9,5},{... | collective-permute-start | bytes 1572872 | tf_op jit(solution)/shard_map/ppermute | solution.py:72
  44.5 0.8 copy-start.2
  45.3 98.5 %reduce-scatter.2.cloned.1.call-start = ((), (), s32[]{:S(2)}) async-start(), calls=%async_computation.2 | async-start | bytes 2621440 | tf_op jit(solution)/shard_map/reduce_scatter | solution.py:80
  85.3 17.6 %copy-start = (f32[512,512]{1,0:T(8,128)S(1)}, f32[512,512]{1,0:T(8,128)}, u32[]{:S(2)}) copy-start(f32[512,512]{1,0:T(8,128)} %param.5) | copy-start | bytes 3145732
  102.6 177.5 %all-reduce.2.cloned.1.call-start = ((), (), s32[]{:S(2)}) async-start(), calls=%async_computation.3 | async-start | bytes 2097152 | tf_op jit(solution)/shard_map/psum | solution.py:83
  143.8 11.2 %copy-start.1 = (bf16[512,512]{1,0:T(8,128)(2,1)S(1)}, bf16[512,512]{1,0:T(8,128)(2,1)}, u32[]{:S(2)}) copy-start(bf16[512,512]{1,0:T(8,128)(2,1)} %reduce-scatter.2.cloned.1.call-done) | copy-start | bytes 1572868
Sparse Core Ops, SparseCore 0:
  45.4 39.7 all-gather.1
  102.8 41.0 reduce-scatter.1
  150.4 129.6 all-reduce.1

commit v2 on v1

--- a/solution.py
+++ b/solution.py
@@ -60,6 +60,219 @@
     )(matrix)
 
 
+MESH = pl.DeviceIdType.MESH
+F32 = jnp.float32
+
+
+def greet(peers):
+    barrier = pltpu.get_barrier_semaphore()
+    for peer in peers:
+        pl.semaphore_signal(barrier, inc=1, device_id=peer, device_id_type=MESH)
+    pl.semaphore_wait(barrier, len(peers))
+
+
+def send(src, dst, send_sem, recv_sem, peer):
+    copy = pltpu.make_async_remote_copy(
+        src_ref=src,
+        dst_ref=dst,
+        send_sem=send_sem,
+        recv_sem=recv_sem,
+        device_id=peer,
+        device_id_type=MESH,
+    )
+    copy.start()
+    return copy
+
+
+def collect_kernel(n_pan, block_ref, out_ref, send_sem, recv_sem, fast_send, fast_recv, own_sem):
+    me = lax.axis_index("panel")
+    chips = n_pan // 2
+    chip, core = me // 2, lax.rem(me, 2)
+    sibling = {"panel": chip * 2 + 1 - core}
+    piece = block_ref.shape[0]
+    greet([sibling] + [{"panel": lax.rem(chip + k, chips) * 2 + core} for k in range(1, chips)])
+
+    def place(index):
+        return out_ref.at[pl.ds(pl.multiple_of(index * piece, piece), piece)]
+
+    slow = []
+    for k in range(1, chips):
+        peer = {"panel": lax.rem(chip + k, chips) * 2 + core}
+        slow.append(send(block_ref, place(me), send_sem.at[k - 1], recv_sem.at[k - 1], peer))
+    fast = [send(block_ref, place(me), fast_send.at[0], fast_recv.at[0], sibling)]
+    own = pltpu.make_async_copy(block_ref, place(me), own_sem)
+    own.start()
+    for k in range(1, chips):
+        slow[k - 1].wait_recv()
+        held = place(lax.rem(chip + chips - k, chips) * 2 + core)
+        fast.append(send(held, held, fast_send.at[k], fast_recv.at[k], sibling))
+    own.wait()
+    for copy in slow:
+        copy.wait_send()
+    for copy in fast:
+        copy.wait()
+
+
+def collect(block):
+    n_pan = lax.axis_size("panel")
+    chips = n_pan // 2
+    piece, width = block.shape
+    return pl.pallas_call(
+        functools.partial(collect_kernel, n_pan),
+        out_shape=jax.ShapeDtypeStruct((n_pan * piece, width), block.dtype),
+        in_specs=[pl.BlockSpec(memory_space=pl.ANY)],
+        out_specs=pl.BlockSpec(memory_space=pl.ANY),
+        scratch_shapes=[
+            pltpu.SemaphoreType.DMA((chips,)),
+            pltpu.SemaphoreType.DMA((chips,)),
+            pltpu.SemaphoreType.DMA((chips,)),
+            pltpu.SemaphoreType.DMA((chips,)),
+            pltpu.SemaphoreType.DMA,
+        ],
+        compiler_params=pltpu.CompilerParams(collective_id=0, has_side_effects=True),
+    )(block)
+
+
+def multiply_kernel(fill_ref, a_ref, columns_ref, out_ref, total):
+    row = pl.program_id(0)
+    total[...] = jnp.zeros_like(total)
+    for j in range(a_ref.shape[1] // B):
+
+        @pl.when(fill_ref[row, j] != 0)
+        def _():
+            total[...] += jnp.dot(
+                a_ref[:, j * B : (j + 1) * B],
+                columns_ref[j * B : (j + 1) * B, :],
+                preferred_element_type=F32,
+            )
+
+    out_ref[...] = total[...].astype(out_ref.dtype)
+
+
+def multiply(fill, adjoint, columns):
+    rows, wide = adjoint.shape
+    width = columns.shape[1]
+    return pl.pallas_call(
+        multiply_kernel,
+        grid=(rows // B,),
+        out_shape=jax.ShapeDtypeStruct((rows, width), jnp.bfloat16),
+        in_specs=[
+            pl.BlockSpec(memory_space=pltpu.SMEM),
+            pl.BlockSpec((B, wide), lambda i: (i, 0)),
+            pl.BlockSpec((wide, width), lambda i: (0, 0)),
+        ],
+        out_specs=pl.BlockSpec((B, width), lambda i: (i, 0)),
+        scratch_shapes=[pltpu.VMEM((B, width), F32)],
+        compiler_params=pltpu.CompilerParams(vmem_limit_bytes=32 * 1024 * 1024),
+        cost_estimate=pl.CostEstimate(
+            flops=2 * rows * wide * width, bytes_accessed=2 * rows * wide, transcendentals=0
+        ),
+    )(fill, adjoint, columns)
+
+
+def halves(x):
+    high = x.astype(jnp.bfloat16)
+    return high, (x - high.astype(F32)).astype(jnp.bfloat16)
+
+
+def dot3(x, y):
+    (xh, xl), (yh, yl) = halves(x), halves(y)
+    mul = functools.partial(jnp.dot, preferred_element_type=F32)
+    return mul(xh, yh) + (mul(xh, yl) + mul(xl, yh))
+
+
+def finish_kernel(
+    n_pan, n_col, part_ref, rows_t_ref, inv_ref, panel_ref, diag_ref,
+    came, summed, quad, quad_came, slab, stacked, full,
+    send0, recv0, send1, recv1, send2, recv2, send3, recv3,
+):
+    pan, col = lax.axis_index("panel"), lax.axis_index("col")
+    pans = [lax.rem(pan + k, n_pan) for k in range(1, n_pan)]
+    cols = [lax.rem(col + k, n_col) for k in range(1, n_col)]
+    piece = came.shape[1]
+    high = slab.shape[0]
+    greet([{"panel": p} for p in pans] + [{"col": c} for c in cols])
+
+    copies = []
+    for k, c in enumerate(cols):
+        src = part_ref.at[pl.ds(pl.multiple_of(c * piece, piece), piece)]
+        copies.append(send(src, came.at[k], send0.at[k], recv0.at[k], {"col": c}))
+    summed[...] = part_ref[pl.ds(pl.multiple_of(col * piece, piece), piece), :].astype(F32)
+    for k in reversed(range(n_col - 1)):
+        copies[k].wait_recv()
+        summed[...] += came[k].astype(F32)
+
+    sum_high, sum_low = halves(summed[...])
+    quad[...] = jnp.dot(rows_t_ref[...], sum_high, preferred_element_type=F32) + jnp.dot(
+        rows_t_ref[...], sum_low, preferred_element_type=F32
+    )
+    for k, p in enumerate(pans):
+        src = quad.at[pl.ds(pl.multiple_of(p * high, high), high)]
+        copies.append(send(src, quad_came.at[k], send1.at[k], recv1.at[k], {"panel": p}))
+    panel_ref[...] = -dot3(summed[...], inv_ref[...])
+    mine = quad[pl.ds(pl.multiple_of(pan * high, high), high), :]
+    for k in range(n_pan - 1):
+        copies[n_col - 1 + k].wait_recv()
+        mine = mine + quad_came[k]
+    slab[...] = mine
+    stacked[col] = mine
+    over_col = []
+    for k, c in enumerate(cols):
+        over_col.append(send(slab, stacked.at[col], send2.at[k], recv2.at[k], {"col": c}))
+    for copy in over_col:
+        copy.wait()
+    total = stacked[0]
+    for c in range(1, n_col):
+        total = total + stacked[c]
+    slab[...] = total
+    here = full.at[pl.ds(pl.multiple_of(pan * high, high), high)]
+    here[...] = total
+    back = []
+    for k, p in enumerate(pans):
+        back.append(send(slab, here, send3.at[k], recv3.at[k], {"panel": p}))
+    for copy in copies:
+        copy.wait_send()
+    for copy in back:
+        copy.wait()
+    inv = inv_ref[...]
+    grown = dot3(inv, dot3(full[...], inv))
+    diag_ref[...] = inv + 0.25 * (grown + grown.T)
+
+
+def finish(part, rows_t, inv):
+    n_pan, n_col = lax.axis_size("panel"), lax.axis_size("col")
+    piece = part.shape[0] // n_col
+    width = part.shape[1]
+    high = width // n_pan
+    vmem = pl.BlockSpec(memory_space=pltpu.VMEM)
+    dma = pltpu.SemaphoreType.DMA
+    return pl.pallas_call(
+        functools.partial(finish_kernel, n_pan, n_col),
+        out_shape=(
+            jax.ShapeDtypeStruct((piece, width), F32),
+            jax.ShapeDtypeStruct((width, width), F32),
+        ),
+        in_specs=[vmem] * 3,
+        out_specs=(vmem, vmem),
+        scratch_shapes=[
+            pltpu.VMEM((n_col - 1, piece, width), jnp.bfloat16),
+            pltpu.VMEM((piece, width), F32),
+            pltpu.VMEM((width, width), F32),
+            pltpu.VMEM((n_pan - 1, high, width), F32),
+            pltpu.VMEM((high, width), F32),
+            pltpu.VMEM((n_col, high, width), F32),
+            pltpu.VMEM((width, width), F32),
+            dma((n_col - 1,)), dma((n_col - 1,)),
+            dma((n_pan - 1,)), dma((n_pan - 1,)),
+            dma((n_col - 1,)), dma((n_col - 1,)),
+            dma((n_pan - 1,)), dma((n_pan - 1,)),
+        ],
+        compiler_params=pltpu.CompilerParams(
+            collective_id=1, has_side_effects=True, vmem_limit_bytes=40 * 1024 * 1024
+        ),
+    )(part, rows_t, inv)
+
+
 def shards(panel_rows, diag_blocks, adjoint, fill):
     n_col = lax.axis_size("col")
     n_pan = lax.axis_size("panel")
@@ -70,24 +283,9 @@
             for z in range(n_col):
                 pairs.append(((groups * c + k) * n_col + z, (k * n_col + z) * n_col + c))
     moved = lax.ppermute(panel_rows, ("panel", "col"), pairs)
-    columns = lax.all_gather(moved, "panel", axis=0, tiled=True)
-    matrix = 0.5 * (diag_blocks + diag_blocks.T)
-    inv = inverse(matrix)
-    marks = jnp.repeat(fill, B, axis=0).astype(jnp.bfloat16)
-    rows, wide = adjoint.shape
-    masked = (adjoint.reshape(rows, wide // B, B) * marks[:, :, None]).reshape(rows, wide)
-    partial = jnp.dot(masked, columns, preferred_element_type=jnp.float32)
-    product = lax.psum_scatter(
-        partial.astype(jnp.bfloat16), "col", scatter_dimension=0, tiled=True
-    )
-    quad = lax.psum(
-        jnp.dot(panel_rows.T, product, preferred_element_type=jnp.float32), ("panel", "col")
-    )
-    grad_panel = -jnp.dot(product.astype(jnp.float32), inv, precision=lax.Precision.HIGH)
-    quad = 0.5 * (quad + quad.T)
-    half = jnp.dot(quad, inv, precision=lax.Precision.HIGH)
-    grad_diag = inv + 0.5 * jnp.dot(inv, half, precision=lax.Precision.HIGH)
-    return (grad_panel, 0.5 * (grad_diag + grad_diag.T))
+    inv = inverse(0.5 * (diag_blocks + diag_blocks.T))
+    part = multiply(fill, adjoint, collect(moved))
+    return finish(part, panel_rows.T, inv)
 
 
 def solution(mesh):

time: 297 us -> 181 us (0.61)
  waiting for transfers between devices: 222 us -> 21.9 us
  Pallas kernels: 8.1 us -> 143 us
  matrix products: 25 us -> 0 us
  between operations: 13.8 us -> 0.71 us
  local copies, waits for them, and re-layouts: 19 us -> 7.74 us
    pallas_call x0 -> x3, Pallas kernels: none -> 135 us  [the longest x1 85.8 us: finish(): pl.pallas_call(functools.partial(finish_kernel, n_pan, n_col), out_shape=...]
    psum x1 -> x0, waiting for transfers between devices: 123 us -> none  [shards(): lax.psum(jnp.dot(panel_rows.T, product, preferred_element_type=jnp.float3...]
    reduce_scatter x1 -> x0, waiting for transfers between devices: 40.4 us -> none  [shards(): lax.psum_scatter(partial.astype(jnp.bfloat16), 'col', scatter_dimension=0...]
    dot_general x5 -> x0, matrix products: 25 us -> none  [the longest x1 17.3 us: shards(): partial = jnp.dot(masked, columns, preferred_element_type=jnp.float32)]
    all_gather x1 -> x0, waiting for transfers between devices: 23.6 us -> none  [shards(): columns = lax.all_gather(moved, 'panel', axis=0, tiled=True)]
    ppermute x1, waiting for transfers between devices: 34.2 us -> 21.9 us  [shards(): moved = lax.ppermute(panel_rows, ('panel', 'col'), pairs)]
    mul x1 -> x0, local copies, waits for them, and re-layouts: 4.93 us -> none  [shards(): adjoint.reshape(rows, wide // B, B) * marks[:, :, None]]
    unnamed x8 -> x10, local copies, waits for them, and re-layouts: 11.8 us -> 7.74 us
  transfers between devices with their start and end apart: 4 -> 1, of which waited for: 4 -> 1; matrix products, arithmetic and copies ran while one was open for 6% -> 2% of each run, Pallas kernels for 3% -> 5%
where the time goes in v2:
time: 181 us; the launch traced here: 178 us
  Pallas kernels  143 us (79%)
  waiting for transfers between devices  21.9 us (12%)
  local copies, waits for them, and re-layouts  7.74 us (4%)
  starting transfers between devices  3.03 us (2%)
    pallas_call x1, Pallas kernels, finish(): pl.pallas_call(functools.partial(finish_kernel, n_pan, n_col), out_shape=...  85.8 us
    pallas_call x1, Pallas kernels, collect(): pl.pallas_call(functools.partial(collect_kernel, n_pan), out_shape=jax.Sh...  28.6 us
    ppermute x1, waiting for transfers between devices, shards(): moved = lax.ppermute(panel_rows, ('panel', 'col'), pairs)  21.9 us
    pallas_call x1, Pallas kernels, multiply(): pl.pallas_call(multiply_kernel, grid=(rows // B,), out_shape=jax.ShapeDty...  20.8 us
    pallas_call x1, Pallas kernels, inverse(): pl.pallas_call(inverse_kernel, out_shape=jax.ShapeDtypeStruct((n, n), jnp...  8.1 us
    unnamed x10, local copies, waits for them, and re-layouts  7.74 us
  transfers between devices with their start and end apart: 1, of which 1 were waited for; matrix products, arithmetic and copies ran while one was open for 2% of the time, Pallas kernels for 5%

profile of v2, /device:TPU:9, one launch (start us, length us, event | category | flops | bytes accessed | tf_op | source)
XLA Modules:
  0.0 178.1 jit_solution(13433017575136894748)
XLA Ops:
  0.6 3.0 %collective-permute-start = (bf16[512,512]{1,0:T(8,128)(2,1)}, bf16[512,512]{1,0:T(8,128)(2,1)S(1)}, u32[]{:S(2)}, u32[]{:S(2)}) collective-permute-start(bf16[512,512]{1,0:T(8,128)(2,1)} %param.4), channel_id=1, source_target_pairs={{0,0},{1,4},{2,8},{3,12},{4,16},{5,20},{6,24},{7,28},{8,1},{9,5},{... | collective-permute-start | bytes 1572872 | tf_op jit(solution)/shard_map/ppermute | solution.py:285
  3.7 1.3 copy.6
  4.9 1.6 copy.7
  6.5 1.4 fusion.matrix_ref
  8.0 8.1 %shard_map.61.inv_ref = f32[512,512]{1,0:T(8,128)S(1)} custom-call(f32[512,512]{1,0:T(8,128)S(1)} %fusion.matrix_ref), custom_call_target="tpu_custom_call" | custom-call | flops 6442450944 | bytes 2097152 | tf_op jit(solution)/shard_map/pallas_call | solution.py:50
  16.1 0.0 copy-start.1
  16.1 21.9 %collective-permute-done.block_ref = bf16[512,512]{1,0:T(8,128)(2,1)S(1)} collective-permute-done((bf16[512,512]{1,0:T(8,128)(2,1)}, bf16[512,512]{1,0:T(8,128)(2,1)S(1)}, u32[]{:S(2)}, u32[]{:S(2)}) %collective-permute-start) | collective-permute-done | bytes 524320 | tf_op jit(solution)/shard_map/ppermute | solution.py:285
  37.9 0.0 copy-start.2
  37.9 0.8 copy-done.2
  38.7 28.6 %shard_map.59.columns_ref = bf16[4096,512]{1,0:T(8,128)(2,1)} custom-call(bf16[512,512]{1,0:T(8,128)(2,1)} %copy-done.2), custom_call_target="tpu_custom_call" | custom-call | tf_op jit(solution)/shard_map/pallas_call | solution.py:120
  67.3 0.0 copy-done.1
  67.3 0.0 copy-start
  67.3 2.2 %copy-done = bf16[4096,512]{1,0:T(8,128)(2,1)S(1)} copy-done((bf16[4096,512]{1,0:T(8,128)(2,1)S(1)}, bf16[4096,512]{1,0:T(8,128)(2,1)}, u32[]{:S(2)}) %copy-start) | copy-done | bytes 4194328
  69.5 20.8 %shard_map.60.part_ref = bf16[2048,512]{1,0:T(8,128)(2,1)S(1)} custom-call(s32[8,16]{1,0:T(8,128)S(1)} %copy-done.1, bf16[2048,4096]{1,0:T(8,128)(2,1)} %a_ref.1, bf16[4096,512]{1,0:T(8,128)(2,1)S(1)} %copy-done), custom_call_target="tpu_custom_call" | custom-call | flops 8589934592 | bytes 16777216 | tf_op jit(solution)/shard_map/pallas_call | solution.py:155
  90.3 85.8 %shard_map.62 = (f32[512,512]{1,0:T(8,128)S(1)}, f32[512,512]{1,0:T(8,128)S(1)}) custom-call(bf16[2048,512]{1,0:T(8,128)(2,1)S(1)} %shard_map.60.part_ref, bf16[512,512]{1,0:T(8,128)(2,1)S(1)} %bitcast.5, f32[512,512]{1,0:T(8,128)S(1)} %shard_map.61.inv_ref), custom_call_target="tpu_custom_call" | custom-call | tf_op jit(solution)/shard_map/pallas_call | solution.py:249
  176.1 1.0 copy.10
  177.1 1.0 copy.11
Async XLA Ops:
  0.6 37.3 %collective-permute-start = (bf16[512,512]{1,0:T(8,128)(2,1)}, bf16[512,512]{1,0:T(8,128)(2,1)S(1)}, u32[]{:S(2)}, u32[]{:S(2)}) collective-permute-start(bf16[512,512]{1,0:T(8,128)(2,1)} %param.4), channel_id=1, source_target_pairs={{0,0},{1,4},{2,8},{3,12},{4,16},{5,20},{6,24},{7,28},{8,1},{9,5},{... | collective-permute-start | bytes 1572872 | tf_op jit(solution)/shard_map/ppermute | solution.py:285
  16.1 51.2 %copy-start.1 = (s32[8,16]{1,0:T(8,128)S(1)}, s32[8,16]{1,0:T(8,128)}, u32[]{:S(2)}) copy-start(s32[8,16]{1,0:T(8,128)} %fill_ref.1) | copy-start | bytes 1540
  37.9 0.8 copy-start.2
  67.3 2.2 %copy-start = (bf16[4096,512]{1,0:T(8,128)(2,1)S(1)}, bf16[4096,512]{1,0:T(8,128)(2,1)}, u32[]{:S(2)}) copy-start(bf16[4096,512]{1,0:T(8,128)(2,1)} %shard_map.59.columns_ref) | copy-start | bytes 12582916

commit v3 on v2

--- a/solution.py
+++ b/solution.py
@@ -133,8 +133,8 @@
     )(block)
 
 
-def multiply_kernel(fill_ref, a_ref, columns_ref, out_ref, total):
-    row = pl.program_id(0)
+def multiply_kernel(start_ref, fill_ref, a_ref, columns_ref, out_ref, total):
+    row = start_ref[0] + pl.program_id(0)
     total[...] = jnp.zeros_like(total)
     for j in range(a_ref.shape[1] // B):
 
@@ -149,25 +149,26 @@
     out_ref[...] = total[...].astype(out_ref.dtype)
 
 
-def multiply(fill, adjoint, columns):
-    rows, wide = adjoint.shape
-    width = columns.shape[1]
+def multiply(start, rows, fill, adjoint, columns):
+    wide, width = columns.shape
     return pl.pallas_call(
         multiply_kernel,
-        grid=(rows // B,),
+        grid_spec=pltpu.PrefetchScalarGridSpec(
+            num_scalar_prefetch=2,
+            grid=(rows // B,),
+            in_specs=[
+                pl.BlockSpec((B, wide), lambda i, s, f: (s[0] + i, 0)),
+                pl.BlockSpec((wide, width), lambda i, s, f: (0, 0)),
+            ],
+            out_specs=pl.BlockSpec((B, width), lambda i, s, f: (i, 0)),
+            scratch_shapes=[pltpu.VMEM((B, width), F32)],
+        ),
         out_shape=jax.ShapeDtypeStruct((rows, width), jnp.bfloat16),
-        in_specs=[
-            pl.BlockSpec(memory_space=pltpu.SMEM),
-            pl.BlockSpec((B, wide), lambda i: (i, 0)),
-            pl.BlockSpec((wide, width), lambda i: (0, 0)),
-        ],
-        out_specs=pl.BlockSpec((B, width), lambda i: (i, 0)),
-        scratch_shapes=[pltpu.VMEM((B, width), F32)],
         compiler_params=pltpu.CompilerParams(vmem_limit_bytes=32 * 1024 * 1024),
         cost_estimate=pl.CostEstimate(
             flops=2 * rows * wide * width, bytes_accessed=2 * rows * wide, transcendentals=0
         ),
-    )(fill, adjoint, columns)
+    )(start, fill, adjoint, columns)
 
 
 def halves(x):
@@ -182,25 +183,23 @@
 
 
 def finish_kernel(
-    n_pan, n_col, part_ref, rows_t_ref, inv_ref, panel_ref, diag_ref,
-    came, summed, quad, quad_came, slab, stacked, full,
-    send0, recv0, send1, recv1, send2, recv2, send3, recv3,
+    n_pan, n_col, *refs
 ):
+    parts, refs = refs[:n_col], refs[n_col:]
+    rows_t_ref, inv_ref, panel_ref, diag_ref, *refs = refs
+    summed, quad, quad_came, slab, stacked, full, *refs = refs
+    send1, recv1, send2, recv2, send3, recv3 = refs
     pan, col = lax.axis_index("panel"), lax.axis_index("col")
     pans = [lax.rem(pan + k, n_pan) for k in range(1, n_pan)]
     cols = [lax.rem(col + k, n_col) for k in range(1, n_col)]
-    piece = came.shape[1]
     high = slab.shape[0]
     greet([{"panel": p} for p in pans] + [{"col": c} for c in cols])
 
     copies = []
-    for k, c in enumerate(cols):
-        src = part_ref.at[pl.ds(pl.multiple_of(c * piece, piece), piece)]
-        copies.append(send(src, came.at[k], send0.at[k], recv0.at[k], {"col": c}))
-    summed[...] = part_ref[pl.ds(pl.multiple_of(col * piece, piece), piece), :].astype(F32)
-    for k in reversed(range(n_col - 1)):
-        copies[k].wait_recv()
-        summed[...] += came[k].astype(F32)
+    total = parts[0][...].astype(F32)
+    for part in parts[1:]:
+        total = total + part[...].astype(F32)
+    summed[...] = total
 
     sum_high, sum_low = halves(summed[...])
     quad[...] = jnp.dot(rows_t_ref[...], sum_high, preferred_element_type=F32) + jnp.dot(
@@ -212,7 +211,7 @@
     panel_ref[...] = -dot3(summed[...], inv_ref[...])
     mine = quad[pl.ds(pl.multiple_of(pan * high, high), high), :]
     for k in range(n_pan - 1):
-        copies[n_col - 1 + k].wait_recv()
+        copies[k].wait_recv()
         mine = mine + quad_came[k]
     slab[...] = mine
     stacked[col] = mine
@@ -239,10 +238,9 @@
     diag_ref[...] = inv + 0.25 * (grown + grown.T)
 
 
-def finish(part, rows_t, inv):
+def finish(parts, rows_t, inv):
     n_pan, n_col = lax.axis_size("panel"), lax.axis_size("col")
-    piece = part.shape[0] // n_col
-    width = part.shape[1]
+    piece, width = parts[0].shape
     high = width // n_pan
     vmem = pl.BlockSpec(memory_space=pltpu.VMEM)
     dma = pltpu.SemaphoreType.DMA
@@ -252,17 +250,15 @@
             jax.ShapeDtypeStruct((piece, width), F32),
             jax.ShapeDtypeStruct((width, width), F32),
         ),
-        in_specs=[vmem] * 3,
+        in_specs=[vmem] * (n_col + 2),
         out_specs=(vmem, vmem),
         scratch_shapes=[
-            pltpu.VMEM((n_col - 1, piece, width), jnp.bfloat16),
             pltpu.VMEM((piece, width), F32),
             pltpu.VMEM((width, width), F32),
             pltpu.VMEM((n_pan - 1, high, width), F32),
             pltpu.VMEM((high, width), F32),
             pltpu.VMEM((n_col, high, width), F32),
             pltpu.VMEM((width, width), F32),
-            dma((n_col - 1,)), dma((n_col - 1,)),
             dma((n_pan - 1,)), dma((n_pan - 1,)),
             dma((n_col - 1,)), dma((n_col - 1,)),
             dma((n_pan - 1,)), dma((n_pan - 1,)),
@@ -270,7 +266,7 @@
         compiler_params=pltpu.CompilerParams(
             collective_id=1, has_side_effects=True, vmem_limit_bytes=40 * 1024 * 1024
         ),
-    )(part, rows_t, inv)
+    )(*parts, rows_t, inv)
 
 
 def shards(panel_rows, diag_blocks, adjoint, fill):
@@ -284,8 +280,17 @@
                 pairs.append(((groups * c + k) * n_col + z, (k * n_col + z) * n_col + c))
     moved = lax.ppermute(panel_rows, ("panel", "col"), pairs)
     inv = inverse(0.5 * (diag_blocks + diag_blocks.T))
-    part = multiply(fill, adjoint, collect(moved))
-    return finish(part, panel_rows.T, inv)
+    columns = collect(moved)
+    piece = panel_rows.shape[0]
+    col = lax.axis_index("col")
+    parts = []
+    for k in range(n_col - 1, -1, -1):
+        start = lax.rem(col + k, n_col) * (piece // B)
+        part = multiply(start.astype(jnp.int32)[None], piece, fill, adjoint, columns)
+        if k:
+            part = lax.ppermute(part, "col", [(c, (c + k) % n_col) for c in range(n_col)])
+        parts.append(part)
+    return finish(parts, panel_rows.T, inv)
 
 
 def solution(mesh):

time: 181 us -> 177 us (0.978); the launches traced: 178 us -> 176 us
  Pallas kernels: 143 us -> 101 us
  local copies, waits for them, and re-layouts: 7.74 us -> 25.7 us
  waiting for transfers between devices: 21.9 us -> 37.1 us
  starting transfers between devices: 3.03 us -> 10.7 us
    pallas_call x1, Pallas kernels: 85.8 us -> 44.7 us  [finish(): pl.pallas_call(functools.partial(finish_kernel, n_pan, n_col), out_shape=...]
    unnamed x10 -> x18, local copies, waits for them, and re-layouts: 7.74 us -> 25.7 us
    ppermute x1, waiting for transfers between devices: 21.9 us -> 30 us  [shards(): moved = lax.ppermute(panel_rows, ('panel', 'col'), pairs)]
    ppermute x0 -> x3, starting transfers between devices: none -> 7.65 us  [shards(): lax.ppermute(part, 'col', [(c, (c + k) % n_col) for c in range(n_col)])]
    ppermute x0 -> x3, waiting for transfers between devices: none -> 7.1 us  [shards(): lax.ppermute(part, 'col', [(c, (c + k) % n_col) for c in range(n_col)])]
    pallas_call x1 -> x4, Pallas kernels: 20.8 us -> 19.3 us  [multiply(): pl.pallas_call(multiply_kernel, grid_spec=pltpu.PrefetchScalarGridSpec(nu...]
  transfers between devices with their start and end apart: 1 -> 4, of which waited for: 1 -> 2; matrix products, arithmetic and copies ran while one was open for 2% -> 2% of each run, Pallas kernels for 5% -> 12%
where the time goes in v3:
time: 177 us; the launch traced here: 176 us
  Pallas kernels  101 us (57%)
  waiting for transfers between devices  37.1 us (21%)
  local copies, waits for them, and re-layouts  25.7 us (15%)
  starting transfers between devices  10.7 us (6%)
    pallas_call x1, Pallas kernels, finish(): pl.pallas_call(functools.partial(finish_kernel, n_pan, n_col), out_shape=...  44.7 us
    ppermute x1, waiting for transfers between devices, shards(): moved = lax.ppermute(panel_rows, ('panel', 'col'), pairs)  30 us
    pallas_call x1, Pallas kernels, collect(): pl.pallas_call(functools.partial(collect_kernel, n_pan), out_shape=jax.Sh...  28.6 us
    unnamed x18, local copies, waits for them, and re-layouts  25.7 us
    pallas_call x4, Pallas kernels, multiply(): pl.pallas_call(multiply_kernel, grid_spec=pltpu.PrefetchScalarGridSpec(nu...  19.3 us
    pallas_call x1, Pallas kernels, inverse(): pl.pallas_call(inverse_kernel, out_shape=jax.ShapeDtypeStruct((n, n), jnp...  8.09 us
    ppermute x3, starting transfers between devices, shards(): lax.ppermute(part, 'col', [(c, (c + k) % n_col) for c in range(n_col)])  7.65 us
    ppermute x3, waiting for transfers between devices, shards(): lax.ppermute(part, 'col', [(c, (c + k) % n_col) for c in range(n_col)])  7.1 us
  transfers between devices with their start and end apart: 4, of which 2 were waited for; matrix products, arithmetic and copies ran while one was open for 2% of the time, Pallas kernels for 12%

profile of v3, /device:TPU:9, one launch (start us, length us, event | category | flops | bytes accessed | tf_op | source)
XLA Modules:
  0.0 176.3 jit_solution(8609012651813120149)
XLA Ops:
  0.6 3.0 %collective-permute-start = (bf16[512,512]{1,0:T(8,128)(2,1)}, bf16[512,512]{1,0:T(8,128)(2,1)S(1)}, u32[]{:S(2)}, u32[]{:S(2)}) collective-permute-start(bf16[512,512]{1,0:T(8,128)(2,1)} %param.4), channel_id=1, source_target_pairs={{0,0},{1,4},{2,8},{3,12},{4,16},{5,20},{6,24},{7,28},{8,1},{9,5},{... | collective-permute-start | bytes 1572872 | tf_op jit(solution)/shard_map/ppermute | solution.py:281
  3.7 1.3 copy.6
  4.9 1.6 copy.7
  6.5 1.4 fusion.matrix_ref
  8.0 30.0 %collective-permute-done.block_ref = bf16[512,512]{1,0:T(8,128)(2,1)S(1)} collective-permute-done((bf16[512,512]{1,0:T(8,128)(2,1)}, bf16[512,512]{1,0:T(8,128)(2,1)S(1)}, u32[]{:S(2)}, u32[]{:S(2)}) %collective-permute-start) | collective-permute-done | bytes 524320 | tf_op jit(solution)/shard_map/ppermute | solution.py:281
  37.9 0.0 copy-start.6
  37.9 0.8 copy-done.6
  38.7 28.6 %shard_map.59.columns_ref = bf16[4096,512]{1,0:T(8,128)(2,1)} custom-call(bf16[512,512]{1,0:T(8,128)(2,1)} %copy-done.6), custom_call_target="tpu_custom_call" | custom-call | tf_op jit(solution)/shard_map/pallas_call | solution.py:120
  67.3 0.0 copy-start
  67.3 5.8 %copy-done = bf16[2048,4096]{1,0:T(8,128)(2,1)S(1)} copy-done((bf16[2048,4096]{1,0:T(8,128)(2,1)S(1)}, bf16[2048,4096]{1,0:T(8,128)(2,1)}, u32[]{:S(2)}) %copy-start) | copy-done | bytes 16777240
  73.1 0.0 copy-start.3
  73.1 2.2 %copy-done.3 = bf16[4096,512]{1,0:T(8,128)(2,1)S(1)} copy-done((bf16[4096,512]{1,0:T(8,128)(2,1)S(1)}, bf16[4096,512]{1,0:T(8,128)(2,1)}, u32[]{:S(2)}) %copy-start.3) | copy-done | bytes 4194328
  75.3 0.7 copy-done.4
  75.9 5.5 %shard_map.61 = bf16[512,512]{1,0:T(8,128)(2,1)S(1)} custom-call(s32[1]{0:T(128)} %bitcast.1.start_ref, s32[8,16]{1,0:T(8,128)S(1)} %copy-done.4, bf16[2048,4096]{1,0:T(8,128)(2,1)S(1)} %copy-done, bf16[4096,512]{1,0:T(8,128)(2,1)S(1)} %copy-done.3), custom_call_target="tpu_custom_call" | custom-call | flops 2147483648 | bytes 4194304 | tf_op jit(solution)/shard_map/pallas_call | solution.py:154
  81.4 5.3 %collective-permute-start.2 = (bf16[512,512]{1,0:T(8,128)(2,1)S(1)}, bf16[512,512]{1,0:T(8,128)(2,1)S(1)}, u32[]{:S(2)}, u32[]{:S(2)}) collective-permute-start(bf16[512,512]{1,0:T(8,128)(2,1)S(1)} %shard_map.61), channel_id=1, source_target_pairs={{0,2},{1,3},{2,0},{3,1},{4,6},{5,7},{6,4},{7,5},{8,10},{9,11},{10,... | collective-permute-start | bytes 1572872 | tf_op jit(solution)/shard_map/ppermute | solution.py:291
  86.7 4.5 %shard_map.62 = bf16[512,512]{1,0:T(8,128)(2,1)S(1)} custom-call(s32[1]{0:T(128)} %bitcast.2.start_ref, s32[8,16]{1,0:T(8,128)S(1)} %copy-done.4, bf16[2048,4096]{1,0:T(8,128)(2,1)S(1)} %copy-done, bf16[4096,512]{1,0:T(8,128)(2,1)S(1)} %copy-done.3), custom_call_target="tpu_custom_call" | custom-call | flops 2147483648 | bytes 4194304 | tf_op jit(solution)/shard_map/pallas_call | solution.py:154
  91.3 0.1 collective-permute-start.3
  91.3 0.0 copy-done.5
  91.3 0.0 copy-start.1
  91.4 5.8 %copy-done.1 = bf16[2048,4096]{1,0:T(8,128)(2,1)S(1)} copy-done((bf16[2048,4096]{1,0:T(8,128)(2,1)S(1)}, bf16[2048,4096]{1,0:T(8,128)(2,1)}, u32[]{:S(2)}) %copy-start.1) | copy-done | bytes 16777240
  97.1 4.6 %shard_map.60 = bf16[512,512]{1,0:T(8,128)(2,1)S(1)} custom-call(s32[1]{0:T(128)} %bitcast.start_ref, s32[8,16]{1,0:T(8,128)S(1)} %copy-done.5, bf16[2048,4096]{1,0:T(8,128)(2,1)S(1)} %copy-done.1, bf16[4096,512]{1,0:T(8,128)(2,1)S(1)} %copy-done.3), custom_call_target="tpu_custom_call" | custom-call | flops 2147483648 | bytes 4194304 | tf_op jit(solution)/shard_map/pallas_call | solution.py:154
  101.7 2.3 %collective-permute-start.1 = (bf16[512,512]{1,0:T(8,128)(2,1)S(1)}, bf16[512,512]{1,0:T(8,128)(2,1)S(1)}, u32[]{:S(2)}, u32[]{:S(2)}) collective-permute-start(bf16[512,512]{1,0:T(8,128)(2,1)S(1)} %shard_map.60), channel_id=1, source_target_pairs={{0,3},{1,0},{2,1},{3,2},{4,7},{5,4},{6,5},{7,6},{8,11},{9,8},{10,9... | collective-permute-start | bytes 1572872 | tf_op jit(solution)/shard_map/ppermute | solution.py:291
  104.0 8.1 %shard_map.64.refs_5_ = f32[512,512]{1,0:T(8,128)S(1)} custom-call(f32[512,512]{1,0:T(8,128)S(1)} %fusion.matrix_ref), custom_call_target="tpu_custom_call" | custom-call | flops 6442450944 | bytes 2097152 | tf_op jit(solution)/shard_map/pallas_call | solution.py:50
  112.1 0.0 copy-start.2
  112.1 5.8 %copy-done.2 = bf16[2048,4096]{1,0:T(8,128)(2,1)S(1)} copy-done((bf16[2048,4096]{1,0:T(8,128)(2,1)S(1)}, bf16[2048,4096]{1,0:T(8,128)(2,1)}, u32[]{:S(2)}) %copy-start.2) | copy-done | bytes 16777240
  117.8 4.7 %shard_map.63.refs_3_ = bf16[512,512]{1,0:T(8,128)(2,1)S(1)} custom-call(s32[1]{0:T(128)} %bitcast.3.start_ref, s32[8,16]{1,0:T(8,128)S(1)} %copy-done.5, bf16[2048,4096]{1,0:T(8,128)(2,1)S(1)} %copy-done.2, bf16[4096,512]{1,0:T(8,128)(2,1)S(1)} %copy-done.3), custom_call_target="tpu_custom_call" | custom-call | flops 2147483648 | bytes 4194304 | tf_op jit(solution)/shard_map/pallas_call | solution.py:154
  122.6 0.0 collective-permute-done.2.refs_1_
  122.6 7.1 %collective-permute-done.3.refs_2_ = bf16[512,512]{1,0:T(8,128)(2,1)S(1)} collective-permute-done((bf16[512,512]{1,0:T(8,128)(2,1)S(1)}, bf16[512,512]{1,0:T(8,128)(2,1)S(1)}, u32[]{:S(2)}, u32[]{:S(2)}) %collective-permute-start.3) | collective-permute-done | bytes 524320 | tf_op jit(solution)/shard_map/ppermute | solution.py:291
  129.7 0.0 collective-permute-done.1.refs_0_
  129.7 44.7 %shard_map.65 = (f32[512,512]{1,0:T(8,128)S(1)}, f32[512,512]{1,0:T(8,128)S(1)}) custom-call(bf16[512,512]{1,0:T(8,128)(2,1)S(1)} %collective-permute-done.1.refs_0_, bf16[512,512]{1,0:T(8,128)(2,1)S(1)} %collective-permute-done.2.refs_1_, bf16[512,512]{1,0:T(8,128)(2,1)S(1)} %collective-permute-done.3.refs_2_, bf16[512,512]{1,0:T(8,128)(2,1)S(1)} %shard_map.63.refs_3_, ...), custom_call_target="tpu_custom_call" | custom-call | tf_op jit(solution)/shard_map/pallas_call | solution.py:247
  174.4 1.0 copy.10
  175.4 1.0 copy.11
  (2 shorter events, 0.0 us)
Async XLA Ops:
  0.6 37.3 %collective-permute-start = (bf16[512,512]{1,0:T(8,128)(2,1)}, bf16[512,512]{1,0:T(8,128)(2,1)S(1)}, u32[]{:S(2)}, u32[]{:S(2)}) collective-permute-start(bf16[512,512]{1,0:T(8,128)(2,1)} %param.4), channel_id=1, source_target_pairs={{0,0},{1,4},{2,8},{3,12},{4,16},{5,20},{6,24},{7,28},{8,1},{9,5},{... | collective-permute-start | bytes 1572872 | tf_op jit(solution)/shard_map/ppermute | solution.py:281
  37.9 0.8 copy-start.6
  67.3 5.8 %copy-start = (bf16[2048,4096]{1,0:T(8,128)(2,1)S(1)}, bf16[2048,4096]{1,0:T(8,128)(2,1)}, u32[]{:S(2)}) copy-start(bf16[2048,4096]{1,0:T(8,128)(2,1)} %a_ref.7) | copy-start | bytes 50331652
  73.1 2.2 %copy-start.3 = (bf16[4096,512]{1,0:T(8,128)(2,1)S(1)}, bf16[4096,512]{1,0:T(8,128)(2,1)}, u32[]{:S(2)}) copy-start(bf16[4096,512]{1,0:T(8,128)(2,1)} %shard_map.59.columns_ref) | copy-start | bytes 12582916
  75.3 0.7 copy-start.4
  75.9 15.4 %copy-start.5 = (s32[8,16]{1,0:T(8,128)S(1)}, s32[8,16]{1,0:T(8,128)}, u32[]{:S(2)}) copy-start(s32[8,16]{1,0:T(8,128)} %fill_ref.7) | copy-start | bytes 1540
  81.4 41.2 %collective-permute-start.2 = (bf16[512,512]{1,0:T(8,128)(2,1)S(1)}, bf16[512,512]{1,0:T(8,128)(2,1)S(1)}, u32[]{:S(2)}, u32[]{:S(2)}) collective-permute-start(bf16[512,512]{1,0:T(8,128)(2,1)S(1)} %shard_map.61), channel_id=1, source_target_pairs={{0,2},{1,3},{2,0},{3,1},{4,6},{5,7},{6,4},{7,5},{8,10},{9,11},{10,... | collective-permute-start | bytes 1572872 | tf_op jit(solution)/shard_map/ppermute | solution.py:291
  91.3 38.4 %collective-permute-start.3 = (bf16[512,512]{1,0:T(8,128)(2,1)S(1)}, bf16[512,512]{1,0:T(8,128)(2,1)S(1)}, u32[]{:S(2)}, u32[]{:S(2)}) collective-permute-start(bf16[512,512]{1,0:T(8,128)(2,1)S(1)} %shard_map.62), channel_id=1, source_target_pairs={{0,1},{1,2},{2,3},{3,0},{4,5},{5,6},{6,7},{7,4},{8,9},{9,10},{10,1... | collective-permute-start | bytes 1572872 | tf_op jit(solution)/shard_map/ppermute | solution.py:291
  91.3 5.8 %copy-start.1 = (bf16[2048,4096]{1,0:T(8,128)(2,1)S(1)}, bf16[2048,4096]{1,0:T(8,128)(2,1)}, u32[]{:S(2)}) copy-start(bf16[2048,4096]{1,0:T(8,128)(2,1)} %a_ref.7) | copy-start | bytes 50331652
  101.7 28.0 %collective-permute-start.1 = (bf16[512,512]{1,0:T(8,128)(2,1)S(1)}, bf16[512,512]{1,0:T(8,128)(2,1)S(1)}, u32[]{:S(2)}, u32[]{:S(2)}) collective-permute-start(bf16[512,512]{1,0:T(8,128)(2,1)S(1)} %shard_map.60), channel_id=1, source_target_pairs={{0,3},{1,0},{2,1},{3,2},{4,7},{5,4},{6,5},{7,6},{8,11},{9,8},{10,9... | collective-permute-start | bytes 1572872 | tf_op jit(solution)/shard_map/ppermute | solution.py:291
  112.1 5.8 %copy-start.2 = (bf16[2048,4096]{1,0:T(8,128)(2,1)S(1)}, bf16[2048,4096]{1,0:T(8,128)(2,1)}, u32[]{:S(2)}) copy-start(bf16[2048,4096]{1,0:T(8,128)(2,1)} %a_ref.7) | copy-start | bytes 50331652

commit v4 on v3

--- a/solution.py
+++ b/solution.py
@@ -164,7 +164,7 @@
             scratch_shapes=[pltpu.VMEM((B, width), F32)],
         ),
         out_shape=jax.ShapeDtypeStruct((rows, width), jnp.bfloat16),
-        compiler_params=pltpu.CompilerParams(vmem_limit_bytes=32 * 1024 * 1024),
+        compiler_params=pltpu.CompilerParams(vmem_limit_bytes=56 * 1024 * 1024),
         cost_estimate=pl.CostEstimate(
             flops=2 * rows * wide * width, bytes_accessed=2 * rows * wide, transcendentals=0
         ),

time: 177 us -> 173 us (0.977)
  local copies, waits for them, and re-layouts: 25.7 us -> 6.59 us
  Pallas kernels: 101 us -> 113 us
    unnamed x18 -> x8, local copies, waits for them, and re-layouts: 25.7 us -> 6.59 us
    pallas_call x4, Pallas kernels: 19.3 us -> 32.4 us  [multiply(): pl.pallas_call(multiply_kernel, grid_spec=pltpu.PrefetchScalarGridSpec(nu...]
  transfers between devices with their start and end apart: 4 -> 4, of which waited for: 2 -> 2; matrix products, arithmetic and copies ran while one was open for 2% -> 2% of each run, Pallas kernels for 12% -> 19%
where the time goes in v4:
time: 173 us; the launch traced here: 172 us
  Pallas kernels  113 us (65%)
  waiting for transfers between devices  38.6 us (22%)
  starting transfers between devices  11.6 us (7%)
  local copies, waits for them, and re-layouts  6.59 us (4%)
    pallas_call x1, Pallas kernels, finish(): pl.pallas_call(functools.partial(finish_kernel, n_pan, n_col), out_shape=...  43.9 us
    pallas_call x4, Pallas kernels, multiply(): pl.pallas_call(multiply_kernel, grid_spec=pltpu.PrefetchScalarGridSpec(nu...  32.4 us
    ppermute x1, waiting for transfers between devices, shards(): moved = lax.ppermute(panel_rows, ('panel', 'col'), pairs)  30 us
    pallas_call x1, Pallas kernels, collect(): pl.pallas_call(functools.partial(collect_kernel, n_pan), out_shape=jax.Sh...  28.6 us
    ppermute x3, waiting for transfers between devices, shards(): lax.ppermute(part, 'col', [(c, (c + k) % n_col) for c in range(n_col)])  8.67 us
    ppermute x3, starting transfers between devices, shards(): lax.ppermute(part, 'col', [(c, (c + k) % n_col) for c in range(n_col)])  8.53 us
    pallas_call x1, Pallas kernels, inverse(): pl.pallas_call(inverse_kernel, out_shape=jax.ShapeDtypeStruct((n, n), jnp...  8.09 us
    unnamed x8, local copies, waits for them, and re-layouts  6.59 us
  transfers between devices with their start and end apart: 4, of which 2 were waited for; matrix products, arithmetic and copies ran while one was open for 2% of the time, Pallas kernels for 19%

profile of v4, /device:TPU:9, one launch (start us, length us, event | category | flops | bytes accessed | tf_op | source)
XLA Modules:
  0.0 171.9 jit_solution(3154371350155185108)
XLA Ops:
  0.6 3.0 %collective-permute-start = (bf16[512,512]{1,0:T(8,128)(2,1)}, bf16[512,512]{1,0:T(8,128)(2,1)S(1)}, u32[]{:S(2)}, u32[]{:S(2)}) collective-permute-start(bf16[512,512]{1,0:T(8,128)(2,1)} %param.4), channel_id=1, source_target_pairs={{0,0},{1,4},{2,8},{3,12},{4,16},{5,20},{6,24},{7,28},{8,1},{9,5},{... | collective-permute-start | bytes 1572872 | tf_op jit(solution)/shard_map/ppermute | solution.py:281
  3.7 1.3 copy.6
  4.9 1.6 copy.7
  6.5 1.4 fusion.matrix_ref
  8.0 30.0 %collective-permute-done.block_ref = bf16[512,512]{1,0:T(8,128)(2,1)S(1)} collective-permute-done((bf16[512,512]{1,0:T(8,128)(2,1)}, bf16[512,512]{1,0:T(8,128)(2,1)S(1)}, u32[]{:S(2)}, u32[]{:S(2)}) %collective-permute-start) | collective-permute-done | bytes 524320 | tf_op jit(solution)/shard_map/ppermute | solution.py:281
  37.9 0.0 copy-start.1
  37.9 0.8 copy-done.1
  38.7 28.6 %shard_map.59.columns_ref = bf16[4096,512]{1,0:T(8,128)(2,1)} custom-call(bf16[512,512]{1,0:T(8,128)(2,1)} %copy-done.1), custom_call_target="tpu_custom_call" | custom-call | tf_op jit(solution)/shard_map/pallas_call | solution.py:120
  67.3 7.3 %shard_map.61 = bf16[512,512]{1,0:T(8,128)(2,1)} custom-call(s32[1]{0:T(128)} %bitcast.1.start_ref, s32[8,16]{1,0:T(8,128)} %fill_ref.7, bf16[2048,4096]{1,0:T(8,128)(2,1)} %a_ref.7, bf16[4096,512]{1,0:T(8,128)(2,1)} %shard_map.59.columns_ref), custom_call_target="tpu_custom_call" | custom-call | flops 2147483648 | bytes 4194304 | tf_op jit(solution)/shard_map/pallas_call | solution.py:154
  74.6 6.2 %collective-permute-start.2 = (bf16[512,512]{1,0:T(8,128)(2,1)}, bf16[512,512]{1,0:T(8,128)(2,1)S(1)}, u32[]{:S(2)}, u32[]{:S(2)}) collective-permute-start(bf16[512,512]{1,0:T(8,128)(2,1)} %shard_map.61), channel_id=1, source_target_pairs={{0,2},{1,3},{2,0},{3,1},{4,6},{5,7},{6,4},{7,5},{8,10},{9,11},{10,... | collective-permute-start | bytes 1572872 | tf_op jit(solution)/shard_map/ppermute | solution.py:291
  80.7 7.7 %shard_map.62 = bf16[512,512]{1,0:T(8,128)(2,1)} custom-call(s32[1]{0:T(128)} %bitcast.2.start_ref, s32[8,16]{1,0:T(8,128)} %fill_ref.7, bf16[2048,4096]{1,0:T(8,128)(2,1)} %a_ref.7, bf16[4096,512]{1,0:T(8,128)(2,1)} %shard_map.59.columns_ref), custom_call_target="tpu_custom_call" | custom-call | flops 2147483648 | bytes 4194304 | tf_op jit(solution)/shard_map/pallas_call | solution.py:154
  88.5 0.0 collective-permute-start.3
  88.5 8.4 %shard_map.60 = bf16[512,512]{1,0:T(8,128)(2,1)} custom-call(s32[1]{0:T(128)} %bitcast.start_ref, s32[8,16]{1,0:T(8,128)} %fill_ref.7, bf16[2048,4096]{1,0:T(8,128)(2,1)} %a_ref.7, bf16[4096,512]{1,0:T(8,128)(2,1)} %shard_map.59.columns_ref), custom_call_target="tpu_custom_call" | custom-call | flops 2147483648 | bytes 4194304 | tf_op jit(solution)/shard_map/pallas_call | solution.py:154
  96.8 2.4 %collective-permute-start.1 = (bf16[512,512]{1,0:T(8,128)(2,1)}, bf16[512,512]{1,0:T(8,128)(2,1)S(1)}, u32[]{:S(2)}, u32[]{:S(2)}) collective-permute-start(bf16[512,512]{1,0:T(8,128)(2,1)} %shard_map.60), channel_id=1, source_target_pairs={{0,3},{1,0},{2,1},{3,2},{4,7},{5,4},{6,5},{7,6},{8,11},{9,8},{10,9... | collective-permute-start | bytes 1572872 | tf_op jit(solution)/shard_map/ppermute | solution.py:291
  99.2 8.1 %shard_map.64.refs_5_ = f32[512,512]{1,0:T(8,128)S(1)} custom-call(f32[512,512]{1,0:T(8,128)S(1)} %fusion.matrix_ref), custom_call_target="tpu_custom_call" | custom-call | flops 6442450944 | bytes 2097152 | tf_op jit(solution)/shard_map/pallas_call | solution.py:50
  107.3 9.1 %shard_map.63.refs_3_ = bf16[512,512]{1,0:T(8,128)(2,1)} custom-call(s32[1]{0:T(128)} %bitcast.3.start_ref, s32[8,16]{1,0:T(8,128)} %fill_ref.7, bf16[2048,4096]{1,0:T(8,128)(2,1)} %a_ref.7, bf16[4096,512]{1,0:T(8,128)(2,1)} %shard_map.59.columns_ref), custom_call_target="tpu_custom_call" | custom-call | flops 2147483648 | bytes 4194304 | tf_op jit(solution)/shard_map/pallas_call | solution.py:154
  116.4 0.0 collective-permute-done.2.refs_1_
  116.4 8.7 %collective-permute-done.3.refs_2_ = bf16[512,512]{1,0:T(8,128)(2,1)S(1)} collective-permute-done((bf16[512,512]{1,0:T(8,128)(2,1)}, bf16[512,512]{1,0:T(8,128)(2,1)S(1)}, u32[]{:S(2)}, u32[]{:S(2)}) %collective-permute-start.3) | collective-permute-done | bytes 524320 | tf_op jit(solution)/shard_map/ppermute | solution.py:291
  125.0 0.0 collective-permute-done.1.refs_0_
  125.0 0.0 copy-start
  125.0 1.0 copy-done
  126.1 43.9 %shard_map.65 = (f32[512,512]{1,0:T(8,128)S(1)}, f32[512,512]{1,0:T(8,128)S(1)}) custom-call(bf16[512,512]{1,0:T(8,128)(2,1)S(1)} %collective-permute-done.1.refs_0_, bf16[512,512]{1,0:T(8,128)(2,1)S(1)} %collective-permute-done.2.refs_1_, bf16[512,512]{1,0:T(8,128)(2,1)S(1)} %collective-permute-done.3.refs_2_, bf16[512,512]{1,0:T(8,128)(2,1)S(1)} %copy-done, ...), custom_call_target="tpu_custom_call" | custom-call | tf_op jit(solution)/shard_map/pallas_call | solution.py:247
  169.9 1.0 copy.10
  170.9 1.0 copy.11
Async XLA Ops:
  0.6 37.3 %collective-permute-start = (bf16[512,512]{1,0:T(8,128)(2,1)}, bf16[512,512]{1,0:T(8,128)(2,1)S(1)}, u32[]{:S(2)}, u32[]{:S(2)}) collective-permute-start(bf16[512,512]{1,0:T(8,128)(2,1)} %param.4), channel_id=1, source_target_pairs={{0,0},{1,4},{2,8},{3,12},{4,16},{5,20},{6,24},{7,28},{8,1},{9,5},{... | collective-permute-start | bytes 1572872 | tf_op jit(solution)/shard_map/ppermute | solution.py:281
  37.9 0.8 copy-start.1
  74.6 41.8 %collective-permute-start.2 = (bf16[512,512]{1,0:T(8,128)(2,1)}, bf16[512,512]{1,0:T(8,128)(2,1)S(1)}, u32[]{:S(2)}, u32[]{:S(2)}) collective-permute-start(bf16[512,512]{1,0:T(8,128)(2,1)} %shard_map.61), channel_id=1, source_target_pairs={{0,2},{1,3},{2,0},{3,1},{4,6},{5,7},{6,4},{7,5},{8,10},{9,11},{10,... | collective-permute-start | bytes 1572872 | tf_op jit(solution)/shard_map/ppermute | solution.py:291
  88.5 36.6 %collective-permute-start.3 = (bf16[512,512]{1,0:T(8,128)(2,1)}, bf16[512,512]{1,0:T(8,128)(2,1)S(1)}, u32[]{:S(2)}, u32[]{:S(2)}) collective-permute-start(bf16[512,512]{1,0:T(8,128)(2,1)} %shard_map.62), channel_id=1, source_target_pairs={{0,1},{1,2},{2,3},{3,0},{4,5},{5,6},{6,7},{7,4},{8,9},{9,10},{10,1... | collective-permute-start | bytes 1572872 | tf_op jit(solution)/shard_map/ppermute | solution.py:291
  96.8 28.2 %collective-permute-start.1 = (bf16[512,512]{1,0:T(8,128)(2,1)}, bf16[512,512]{1,0:T(8,128)(2,1)S(1)}, u32[]{:S(2)}, u32[]{:S(2)}) collective-permute-start(bf16[512,512]{1,0:T(8,128)(2,1)} %shard_map.60), channel_id=1, source_target_pairs={{0,3},{1,0},{2,1},{3,2},{4,7},{5,4},{6,5},{7,6},{8,11},{9,8},{10,9... | collective-permute-start | bytes 1572872 | tf_op jit(solution)/shard_map/ppermute | solution.py:291
  125.0 1.0 copy-start

commit v5 on v4

--- a/solution.py
+++ b/solution.py
@@ -202,17 +202,18 @@
     summed[...] = total
 
     sum_high, sum_low = halves(summed[...])
-    quad[...] = jnp.dot(rows_t_ref[...], sum_high, preferred_element_type=F32) + jnp.dot(
+    own = jnp.dot(rows_t_ref[...], sum_high, preferred_element_type=F32) + jnp.dot(
         rows_t_ref[...], sum_low, preferred_element_type=F32
     )
+    quad[...] = own.astype(quad.dtype)
     for k, p in enumerate(pans):
         src = quad.at[pl.ds(pl.multiple_of(p * high, high), high)]
         copies.append(send(src, quad_came.at[k], send1.at[k], recv1.at[k], {"panel": p}))
     panel_ref[...] = -dot3(summed[...], inv_ref[...])
-    mine = quad[pl.ds(pl.multiple_of(pan * high, high), high), :]
+    mine = quad[pl.ds(pl.multiple_of(pan * high, high), high), :].astype(F32)
     for k in range(n_pan - 1):
         copies[k].wait_recv()
-        mine = mine + quad_came[k]
+        mine = mine + quad_came[k].astype(F32)
     slab[...] = mine
     stacked[col] = mine
     over_col = []
@@ -254,8 +255,8 @@
         out_specs=(vmem, vmem),
         scratch_shapes=[
             pltpu.VMEM((piece, width), F32),
-            pltpu.VMEM((width, width), F32),
-            pltpu.VMEM((n_pan - 1, high, width), F32),
+            pltpu.VMEM((width, width), jnp.bfloat16),
+            pltpu.VMEM((n_pan - 1, high, width), jnp.bfloat16),
             pltpu.VMEM((high, width), F32),
             pltpu.VMEM((n_col, high, width), F32),
             pltpu.VMEM((width, width), F32),

time: 173 us -> 169 us (0.977)
  Pallas kernels: 113 us -> 109 us
    pallas_call x1, Pallas kernels: 43.9 us -> 39.8 us  [finish(): pl.pallas_call(functools.partial(finish_kernel, n_pan, n_col), out_shape=...]
  transfers between devices with their start and end apart: 4 -> 4, of which waited for: 2 -> 2; matrix products, arithmetic and copies ran while one was open for 2% -> 3% of each run, Pallas kernels for 19% -> 19%
where the time goes in v5:
time: 169 us; the launch traced here: 168 us
  Pallas kernels  109 us (64%)
  waiting for transfers between devices  38 us (22%)
  starting transfers between devices  11.5 us (7%)
  local copies, waits for them, and re-layouts  6.59 us (4%)
    pallas_call x1, Pallas kernels, finish(): pl.pallas_call(functools.partial(finish_kernel, n_pan, n_col), out_shape=...  39.8 us
    pallas_call x4, Pallas kernels, multiply(): pl.pallas_call(multiply_kernel, grid_spec=pltpu.PrefetchScalarGridSpec(nu...  32.9 us
    ppermute x1, waiting for transfers between devices, shards(): moved = lax.ppermute(panel_rows, ('panel', 'col'), pairs)  30 us
    pallas_call x1, Pallas kernels, collect(): pl.pallas_call(functools.partial(collect_kernel, n_pan), out_shape=jax.Sh...  28.6 us
    ppermute x3, starting transfers between devices, shards(): lax.ppermute(part, 'col', [(c, (c + k) % n_col) for c in range(n_col)])  8.45 us
    pallas_call x1, Pallas kernels, inverse(): pl.pallas_call(inverse_kernel, out_shape=jax.ShapeDtypeStruct((n, n), jnp...  8.09 us
    ppermute x3, waiting for transfers between devices, shards(): lax.ppermute(part, 'col', [(c, (c + k) % n_col) for c in range(n_col)])  8 us
    unnamed x8, local copies, waits for them, and re-layouts  6.59 us
  transfers between devices with their start and end apart: 4, of which 2 were waited for; matrix products, arithmetic and copies ran while one was open for 3% of the time, Pallas kernels for 19%

profile of v5, /device:TPU:9, one launch (start us, length us, event | category | flops | bytes accessed | tf_op | source)
XLA Modules:
  0.0 167.6 jit_solution(7651978082360933279)
XLA Ops:
  0.6 3.0 %collective-permute-start = (bf16[512,512]{1,0:T(8,128)(2,1)}, bf16[512,512]{1,0:T(8,128)(2,1)S(1)}, u32[]{:S(2)}, u32[]{:S(2)}) collective-permute-start(bf16[512,512]{1,0:T(8,128)(2,1)} %param.4), channel_id=1, source_target_pairs={{0,0},{1,4},{2,8},{3,12},{4,16},{5,20},{6,24},{7,28},{8,1},{9,5},{... | collective-permute-start | bytes 1572872 | tf_op jit(solution)/shard_map/ppermute | solution.py:282
  3.7 1.3 copy.6
  4.9 1.6 copy.7
  6.5 1.4 fusion.matrix_ref
  8.0 30.0 %collective-permute-done.block_ref = bf16[512,512]{1,0:T(8,128)(2,1)S(1)} collective-permute-done((bf16[512,512]{1,0:T(8,128)(2,1)}, bf16[512,512]{1,0:T(8,128)(2,1)S(1)}, u32[]{:S(2)}, u32[]{:S(2)}) %collective-permute-start) | collective-permute-done | bytes 524320 | tf_op jit(solution)/shard_map/ppermute | solution.py:282
  37.9 0.0 copy-start.1
  37.9 0.8 copy-done.1
  38.7 28.6 %shard_map.59.columns_ref = bf16[4096,512]{1,0:T(8,128)(2,1)} custom-call(bf16[512,512]{1,0:T(8,128)(2,1)} %copy-done.1), custom_call_target="tpu_custom_call" | custom-call | tf_op jit(solution)/shard_map/pallas_call | solution.py:120
  67.3 8.9 %shard_map.61 = bf16[512,512]{1,0:T(8,128)(2,1)} custom-call(s32[1]{0:T(128)} %bitcast.1.start_ref, s32[8,16]{1,0:T(8,128)} %fill_ref.7, bf16[2048,4096]{1,0:T(8,128)(2,1)} %a_ref.7, bf16[4096,512]{1,0:T(8,128)(2,1)} %shard_map.59.columns_ref), custom_call_target="tpu_custom_call" | custom-call | flops 2147483648 | bytes 4194304 | tf_op jit(solution)/shard_map/pallas_call | solution.py:154
  76.1 5.0 %collective-permute-start.2 = (bf16[512,512]{1,0:T(8,128)(2,1)}, bf16[512,512]{1,0:T(8,128)(2,1)S(1)}, u32[]{:S(2)}, u32[]{:S(2)}) collective-permute-start(bf16[512,512]{1,0:T(8,128)(2,1)} %shard_map.61), channel_id=1, source_target_pairs={{0,2},{1,3},{2,0},{3,1},{4,6},{5,7},{6,4},{7,5},{8,10},{9,11},{10,... | collective-permute-start | bytes 1572872 | tf_op jit(solution)/shard_map/ppermute | solution.py:292
  81.2 9.3 %shard_map.62 = bf16[512,512]{1,0:T(8,128)(2,1)} custom-call(s32[1]{0:T(128)} %bitcast.2.start_ref, s32[8,16]{1,0:T(8,128)} %fill_ref.7, bf16[2048,4096]{1,0:T(8,128)(2,1)} %a_ref.7, bf16[4096,512]{1,0:T(8,128)(2,1)} %shard_map.59.columns_ref), custom_call_target="tpu_custom_call" | custom-call | flops 2147483648 | bytes 4194304 | tf_op jit(solution)/shard_map/pallas_call | solution.py:154
  90.5 0.0 collective-permute-start.3
  90.5 6.8 %shard_map.60 = bf16[512,512]{1,0:T(8,128)(2,1)} custom-call(s32[1]{0:T(128)} %bitcast.start_ref, s32[8,16]{1,0:T(8,128)} %fill_ref.7, bf16[2048,4096]{1,0:T(8,128)(2,1)} %a_ref.7, bf16[4096,512]{1,0:T(8,128)(2,1)} %shard_map.59.columns_ref), custom_call_target="tpu_custom_call" | custom-call | flops 2147483648 | bytes 4194304 | tf_op jit(solution)/shard_map/pallas_call | solution.py:154
  97.3 3.4 %collective-permute-start.1 = (bf16[512,512]{1,0:T(8,128)(2,1)}, bf16[512,512]{1,0:T(8,128)(2,1)S(1)}, u32[]{:S(2)}, u32[]{:S(2)}) collective-permute-start(bf16[512,512]{1,0:T(8,128)(2,1)} %shard_map.60), channel_id=1, source_target_pairs={{0,3},{1,0},{2,1},{3,2},{4,7},{5,4},{6,5},{7,6},{8,11},{9,8},{10,9... | collective-permute-start | bytes 1572872 | tf_op jit(solution)/shard_map/ppermute | solution.py:292
  100.7 8.1 %shard_map.64.refs_5_ = f32[512,512]{1,0:T(8,128)S(1)} custom-call(f32[512,512]{1,0:T(8,128)S(1)} %fusion.matrix_ref), custom_call_target="tpu_custom_call" | custom-call | flops 6442450944 | bytes 2097152 | tf_op jit(solution)/shard_map/pallas_call | solution.py:50
  108.8 8.0 %shard_map.63.refs_3_ = bf16[512,512]{1,0:T(8,128)(2,1)} custom-call(s32[1]{0:T(128)} %bitcast.3.start_ref, s32[8,16]{1,0:T(8,128)} %fill_ref.7, bf16[2048,4096]{1,0:T(8,128)(2,1)} %a_ref.7, bf16[4096,512]{1,0:T(8,128)(2,1)} %shard_map.59.columns_ref), custom_call_target="tpu_custom_call" | custom-call | flops 2147483648 | bytes 4194304 | tf_op jit(solution)/shard_map/pallas_call | solution.py:154
  116.8 0.0 collective-permute-done.2.refs_1_
  116.8 8.0 %collective-permute-done.3.refs_2_ = bf16[512,512]{1,0:T(8,128)(2,1)S(1)} collective-permute-done((bf16[512,512]{1,0:T(8,128)(2,1)}, bf16[512,512]{1,0:T(8,128)(2,1)S(1)}, u32[]{:S(2)}, u32[]{:S(2)}) %collective-permute-start.3) | collective-permute-done | bytes 524320 | tf_op jit(solution)/shard_map/ppermute | solution.py:292
  124.8 0.0 collective-permute-done.1.refs_0_
  124.8 0.0 copy-start
  124.8 1.0 copy-done
  125.8 39.8 %shard_map.65 = (f32[512,512]{1,0:T(8,128)S(1)}, f32[512,512]{1,0:T(8,128)S(1)}) custom-call(bf16[512,512]{1,0:T(8,128)(2,1)S(1)} %collective-permute-done.1.refs_0_, bf16[512,512]{1,0:T(8,128)(2,1)S(1)} %collective-permute-done.2.refs_1_, bf16[512,512]{1,0:T(8,128)(2,1)S(1)} %collective-permute-done.3.refs_2_, bf16[512,512]{1,0:T(8,128)(2,1)S(1)} %copy-done, ...), custom_call_target="tpu_custom_call" | custom-call | tf_op jit(solution)/shard_map/pallas_call | solution.py:248
  165.6 1.0 copy.10
  166.6 1.0 copy.11
Async XLA Ops:
  0.6 37.3 %collective-permute-start = (bf16[512,512]{1,0:T(8,128)(2,1)}, bf16[512,512]{1,0:T(8,128)(2,1)S(1)}, u32[]{:S(2)}, u32[]{:S(2)}) collective-permute-start(bf16[512,512]{1,0:T(8,128)(2,1)} %param.4), channel_id=1, source_target_pairs={{0,0},{1,4},{2,8},{3,12},{4,16},{5,20},{6,24},{7,28},{8,1},{9,5},{... | collective-permute-start | bytes 1572872 | tf_op jit(solution)/shard_map/ppermute | solution.py:282
  37.9 0.8 copy-start.1
  76.1 40.6 %collective-permute-start.2 = (bf16[512,512]{1,0:T(8,128)(2,1)}, bf16[512,512]{1,0:T(8,128)(2,1)S(1)}, u32[]{:S(2)}, u32[]{:S(2)}) collective-permute-start(bf16[512,512]{1,0:T(8,128)(2,1)} %shard_map.61), channel_id=1, source_target_pairs={{0,2},{1,3},{2,0},{3,1},{4,6},{5,7},{6,4},{7,5},{8,10},{9,11},{10,... | collective-permute-start | bytes 1572872 | tf_op jit(solution)/shard_map/ppermute | solution.py:292
  90.5 34.3 %collective-permute-start.3 = (bf16[512,512]{1,0:T(8,128)(2,1)}, bf16[512,512]{1,0:T(8,128)(2,1)S(1)}, u32[]{:S(2)}, u32[]{:S(2)}) collective-permute-start(bf16[512,512]{1,0:T(8,128)(2,1)} %shard_map.62), channel_id=1, source_target_pairs={{0,1},{1,2},{2,3},{3,0},{4,5},{5,6},{6,7},{7,4},{8,9},{9,10},{10,1... | collective-permute-start | bytes 1572872 | tf_op jit(solution)/shard_map/ppermute | solution.py:292
  97.3 27.5 %collective-permute-start.1 = (bf16[512,512]{1,0:T(8,128)(2,1)}, bf16[512,512]{1,0:T(8,128)(2,1)S(1)}, u32[]{:S(2)}, u32[]{:S(2)}) collective-permute-start(bf16[512,512]{1,0:T(8,128)(2,1)} %shard_map.60), channel_id=1, source_target_pairs={{0,3},{1,0},{2,1},{3,2},{4,7},{5,4},{6,5},{7,6},{8,11},{9,8},{10,9... | collective-permute-start | bytes 1572872 | tf_op jit(solution)/shard_map/ppermute | solution.py:292
  124.8 1.0 copy-start
